TPU v7x, 32 devices: a whole 2x2x4 slice. The times are simulated.
32 devices in a mesh: cuts: 2 (over y), samp: 2 (over core), blk: 4 (over z), tile: 2 (over x).
Axes of the slice: x: 2, y: 2, z: 4, core: 2. Of those that a mesh axis runs over, the one named last changes fastest.
Arguments:
- residual: bfloat16 [2, 4096, 2, 512], P('samp', ('cuts', 'blk', 'tile')), parts along dimension 1, may hold values from -0.25 to 0.25
- uv_offsets: float32 [4096, 2, 512], P(('cuts', 'blk', 'tile')), parts along dimension 0, may hold values from -16 to 16
- counts: int32 [4096], P(('cuts', 'blk', 'tile')), parts along dimension 0, may hold values from 128 to 512
- tile_of_block: int32 [4096, 1], P(('cuts', 'blk', 'tile')), parts along dimension 0, may hold values from 0 to 7; in each aligned block of 256 rows (0 to 255, 256 to 511, ...) at most 64 rows name the same one
- slot_of_block: int32 [4096], P(('cuts', 'blk', 'tile')), parts along dimension 0, may hold values from 0 to 127
- owner_map: int32 [8], replicated, may hold values from 0 to 7, each once
Outputs:
- grid_tiles: float32 [512, 2, 4096], P(('cuts', 'blk', 'tile')), parts along dimension 0
There are 2 independent parts, one for each index of `cuts`. A program takes and returns all parts, laid end to end along the dimension named above; an argument that names none is the same for every part. Nothing has to cross between parts.
Inputs may be any that keep to these rules, and one draw needn't show every extreme that they name: `tile_of_block`: in the rows of one device, no tile is named by more than 64 blocks; some tile is named by exactly 64. `owner_map`: each tile has one owner and each owner one tile.
All inputs are finite; a program needn't handle non-finite values.
Results may differ from a plain program's by a relative error of at most 0.0047.
Values may be sent and summed in bfloat16 or wider, within the bound.
No kernel may reach another device: no remote copies, remote signals or barrier semaphores. Data moves between devices by JAX's collectives and lax.ppermute only.
A program may use at most 64 MiB of HBM per device.

v0:
```python
import functools

import jax
import jax.numpy as jnp
import numpy as np
from jax import lax
from jax.experimental import pallas as pl
from jax.experimental.layout import Layout, with_layout_constraint
from jax.experimental.pallas import tpu as pltpu
from jax.sharding import PartitionSpec as P

SUB = 32
STEPS = SUB // 2
SLOTS = 128
LANES = 128
FEATURE = 2 * SUB * SUB
PIECES = FEATURE // LANES
CAP_MIN = 8
GROUP = 8
QUAD = 4
TAG_ROWS = 16
COUNT_BITS = 12
TAG_BITS = 8
CHUNK = 4 * LANES
PAIRED_MAX = 16
CALLS = (0, 2, 5, 7, 8)
VMEM_LIMIT = 48 * 1024 * 1024


def turn_coefficients():
    knots = np.cos(np.pi * (np.arange(400) + 0.5) / 400)
    cheb = np.polynomial.chebyshev
    even = cheb.cheb2poly(cheb.chebfit(knots, np.cos(np.pi * knots), 12))[0::2]
    odd = cheb.cheb2poly(cheb.chebfit(knots, np.sin(np.pi * knots), 13))[1::2]
    return [float(x) for x in even], [float(x) for x in odd]


COS_COEF, SIN_COEF = turn_coefficients()


def horner(coef, x):
    total = coef[-1] * x + coef[-2]
    for value in coef[-3::-1]:
        total = total * x + value
    return total


def first_angle(offset):
    y = offset * (1.0 / STEPS)
    x = y * y
    return horner(COS_COEF, x), horner(SIN_COEF, x) * y


def tile_of(value, t):
    return value[:, t * LANES : (t + 1) * LANES]


def by_quad(even, odd):
    top = lax.broadcasted_iota(jnp.int32, even.shape, 0) < QUAD
    return (
        jnp.where(top, even, pltpu.roll(odd, QUAD, 0)),
        jnp.where(top, pltpu.roll(even, QUAD, 0), odd),
    )


def sequence(before, middle, factor):
    def pair(*two):
        return jnp.concatenate(two, 0).astype(jnp.bfloat16)

    up, down = [], []
    last, value = before, middle
    for _ in range(STEPS // 4):
        after = factor * value - last
        up.append(pair(value, after))
        last, value = after, factor * after - value
    last, value = middle, before
    for _ in range(STEPS // 4):
        after = factor * value - last
        down.append(pair(after, value))
        last, value = after, factor * after - value
    return down[::-1] + up


def subgrid_kernel(
    first, destinations, capacity, listed, plan_ref, token_ref, uv_ref, res_ref, *refs
):
    out_refs, (next_ref, gathered, recent, found, tags, mover) = refs[:-6], refs[-6:]
    next_ref[...] = jnp.zeros_like(next_ref)
    tiles = gathered.shape[0] // (4 * GROUP)
    spare = destinations * capacity // QUAD

    def start_of(destination):
        return plan_ref[2 * listed + destination]

    low, high = start_of(first), start_of(first + destinations)
    last = listed - 1
    vis_at = lax.broadcasted_iota(jnp.int32, (2 * tiles, LANES), 1) + LANES * (
        lax.broadcasted_iota(jnp.int32, (2 * tiles, LANES), 0) >> 1
    )
    same_block = (
        lax.broadcasted_iota(jnp.int32, (GROUP, LANES), 0) & (QUAD - 1)
        == lax.broadcasted_iota(jnp.int32, (GROUP, LANES), 1) & (QUAD - 1)
    )
    quad_row = lax.broadcasted_iota(jnp.int32, (QUAD, LANES), 0)
    top = lax.broadcasted_iota(jnp.int32, (GROUP, LANES), 0) < QUAD

    source = lax.broadcasted_iota(jnp.int32, mover.shape, 0)
    lane = lax.broadcasted_iota(jnp.int32, mover.shape, 1)
    moves = (source >> 7 == lane >> 5) & ((source & (LANES - 1)) >> 2 == lane & (SUB - 1))
    mover[...] = jnp.where(moves, 1.0, 0.0).astype(jnp.bfloat16)
    tags[...] = jnp.zeros_like(tags)

    def angles(quad_at):
        for i in range(GROUP):
            packed = plan_ref[jnp.minimum(quad_at * QUAD + i, last)]
            block, count = packed >> COUNT_BITS, packed & ((1 << COUNT_BITS) - 1)
            at = pl.ds(pl.multiple_of(block * 2 * tiles, 2 * tiles), 2 * tiles)
            both = jnp.where(vis_at < count, res_ref[at, :], 0.0)
            gathered[pl.ds(i, 2 * tiles, stride=GROUP), :] = uv_ref[at, :]
            gathered[pl.ds(2 * tiles * GROUP + i, 2 * tiles, stride=GROUP), :] = both
        u, v, re, im = [
            jnp.concatenate(
                [
                    gathered[pl.ds(((k // 2) * 2 * tiles + 2 * t + k % 2) * GROUP, GROUP), :]
                    for t in range(tiles)
                ],
                1,
            )
            for k in range(4)
        ]
        c, s = first_angle(u)
        a, b, e, f = re * c, im * s, im * c, re * s
        after = (a - b, e + f)
        before = (a + b, e - f)
        second = [2.0 * c * near - far for near, far in zip(before, (re, im))]
        factor = 2.0 - 4.0 * s * s
        left_factor = by_quad(factor, factor)
        left = [(by_quad(x, y), by_quad(z, w)) for x, y, z, w in zip(second, before, (re, im), after)]
        c, s = first_angle(v)
        c2, s2 = 1.0 - 2.0 * s * s, 2.0 * s * c
        factor = 2.0 * c2
        right_factor = by_quad(factor, factor)
        right = [
            (by_quad(c2, c), by_quad(jnp.ones_like(c), c)),
            (by_quad(-s2, -s), by_quad(jnp.zeros_like(s), s)),
        ]
        return [
            [
                (left[0][0][q], left[0][1][q], left[1][0][q], left[1][1][q], left_factor[q]),
                (right[0][0][q], right[0][1][q], right[1][0][q], right[1][1][q], right_factor[q]),
            ]
            for q in range(2)
        ]

    def place_of(quad_at):
        index = jnp.clip(quad_at * QUAD, 0, last + 1 - QUAD)
        place = (plan_ref[listed + index] >> (TAG_BITS + 2)) - first * (capacity // QUAD)
        return index, jnp.where((quad_at >= low) & (quad_at < high), place, spare)

    def settle(quad_at):
        moved = jnp.dot(recent[...], mover[...], preferred_element_type=jnp.float32)
        for q in range(2):
            _, place = place_of(quad_at + q)
            found[place] = moved[q * found.shape[1] : (q + 1) * found.shape[1]]

    def finish(seeds, quad_at, q):
        product = None
        for lanes in range(0, tiles * LANES, CHUNK):
            operands = []
            for side in seeds[::-1]:
                before, middle, before_imag, middle_imag, factor = [
                    x[:, lanes : lanes + CHUNK] for x in side
                ]
                operands.append(
                    jnp.concatenate(
                        sequence(before, middle, factor)
                        + sequence(before_imag, middle_imag, factor),
                        0,
                    )
                )
            term = lax.dot_general(
                operands[1], operands[0], (((1,), (1,)), ((), ())),
                preferred_element_type=jnp.float32,
            )
            product = term if product is None else product + term
        half = product.shape[0] // 2
        wholes = (
            product[:half, :LANES] - product[half:, LANES:],
            product[half:, :LANES] + product[:half, LANES:],
        )
        rows = []
        for whole in wholes:
            for j in range(0, STEPS, 4):
                four = [whole[(j + k) * GROUP : (j + k + 1) * GROUP] for k in range(4)]
                rows.append(jnp.concatenate([jnp.where(same_block, x, 0.0) for x in four], 1))
        size = found.shape[1]
        recent[pl.ds(q * size, size), :] = jnp.concatenate(rows, 0).astype(jnp.bfloat16)
        index, place = place_of(quad_at)
        tag = jnp.zeros((QUAD, LANES), jnp.int32)
        for b in range(QUAD):
            tag = jnp.where(quad_row == b, plan_ref[listed + index + b] & ((1 << TAG_BITS) - 1), tag)
        tags[place] = tag.astype(jnp.float32)

    def turn(g, seeds):
        quad_at = low + 2 * g
        settle(quad_at - 2)
        for q in range(2):
            finish(seeds[q], quad_at + q, q)
        return angles(quad_at + 2)

    turns = (high - low + 1) >> 1
    lax.fori_loop(0, turns, turn, angles(low))
    settle(low + 2 * turns - 2)

    shares = capacity // TAG_ROWS
    share = lax.broadcasted_iota(jnp.int32, (TAG_ROWS, LANES), 1) // (LANES // shares)

    def write_share(out_ref, base, slot, sent, n):
        for piece in range(PIECES // 2):
            part = []
            for k in range(4):
                value = found[slot + k, pl.ds(piece * GROUP, GROUP), :]
                part.append(jnp.where(n * 4 + k < sent, value, 0.0))
            first_two, last_two = [], []
            for even, odd in (part[:2], part[2:]):
                first_two.append(jnp.where(top, even, pltpu.roll(odd, QUAD, 0)))
                last_two.append(jnp.where(top, pltpu.roll(even, QUAD, 0), odd))
            for parity, two in enumerate((first_two, last_two)):
                put = base + (piece * 2 + parity) * capacity + n * TAG_ROWS
                out_ref[pl.ds(put, TAG_ROWS), :] = jnp.concatenate(two, 0).astype(jnp.bfloat16)

    for d, out_ref in enumerate(out_refs):
        for m in range(out_ref.shape[0] // message_rows(capacity)):
            base = m * message_rows(capacity)
            sent = start_of(first + d + m + 1) - start_of(first + d + m)
            slot = (d + m) * (capacity // QUAD)
            tag = jnp.zeros((TAG_ROWS, LANES), jnp.float32)
            for n in range(shares):
                at = slot + n * 4
                four = jnp.concatenate([tags[at + k] for k in range(4)], 0)
                tag = jnp.where(share == n, four, tag)
                write_share(out_ref, base, at, sent, n)
            out_ref[pl.ds(base + PIECES * capacity, TAG_ROWS), :] = tag.astype(jnp.bfloat16)


def message_rows(capacity):
    return PIECES * capacity + TAG_ROWS


def make_subgrids(first, outs, token, capacity, listed, plan, uv, res, vis):
    tiles = vis // LANES
    destinations = sum(outs)
    quads = destinations * capacity // QUAD
    vmem = pl.BlockSpec(memory_space=pltpu.VMEM)
    smem = pl.BlockSpec(memory_space=pltpu.SMEM)
    return pl.pallas_call(
        functools.partial(subgrid_kernel, first, destinations, capacity, listed),
        out_shape=[
            jax.ShapeDtypeStruct((n * message_rows(capacity), LANES), jnp.bfloat16) for n in outs
        ]
        + [jax.ShapeDtypeStruct(token.shape, token.dtype)],
        in_specs=[smem] + [vmem] * 3,
        out_specs=[vmem] * (len(outs) + 1),
        scratch_shapes=[
            pltpu.VMEM((4 * tiles * GROUP, LANES), jnp.float32),
            pltpu.VMEM((2 * FEATURE // SUB, 4 * LANES), jnp.bfloat16),
            pltpu.VMEM((quads + 1, FEATURE // SUB, LANES), jnp.float32),
            pltpu.VMEM((quads + 1, QUAD, LANES), jnp.float32),
            pltpu.VMEM((4 * LANES, LANES), jnp.bfloat16),
        ],
        compiler_params=pltpu.CompilerParams(vmem_limit_bytes=VMEM_LIMIT),
        cost_estimate=pl.CostEstimate(
            flops=quads * 32 * SUB * SUB * vis, bytes_accessed=16 * quads * FEATURE, transcendentals=0
        ),
        name="subgrids",
    )(plan, token, uv, res)


def pick_rows(hot, xs, part, out_ref, half):
    lane = lax.broadcasted_iota(jnp.int32, (GROUP, LANES), 1) >> 5
    for piece in range(PIECES):
        c, rows, parity = piece // 8, piece // 2 % 4 - 2 * half, piece % 2
        if not 0 <= rows < 2:
            continue
        part[...] = jnp.dot(hot[...], xs[piece], preferred_element_type=jnp.float32)
        for grp in range(4):
            given = [part[pl.ds(32 * jl + 8 * grp, 8), :] for jl in range(4)]
            for a in range(4):
                total = None
                for jl in range(4):
                    moved = given[jl]
                    if a != jl:
                        moved = pltpu.roll(moved, ((jl - a) % 4) * SUB, 1)
                    total = moved if total is None else jnp.where(lane == jl, moved, total)
                p = rows * 8 + a * 2 + parity
                out_ref[pl.ds(p * 64 + grp * 16 + c, 8, stride=2), :] = total


def first_half_kernel(capacity, *refs):
    x_refs, (out_ref, xs, hot, tags, part) = refs[:-5], refs[-5:]
    shares = capacity // TAG_ROWS
    at = 0
    for x_ref in x_refs:
        for base in range(0, x_ref.shape[0], message_rows(capacity)):
            for piece in range(PIECES):
                xs[piece, pl.ds(at, capacity), :] = x_ref[pl.ds(base + piece * capacity, capacity), :]
            tag = x_ref[pl.ds(base + PIECES * capacity, TAG_ROWS), :].astype(jnp.float32)
            for n in range(shares):
                column = n * (LANES // shares)
                tags[pl.ds(at + n * TAG_ROWS, TAG_ROWS), :] = jnp.broadcast_to(
                    tag[:, column : column + 1], (TAG_ROWS, LANES)
                )
            at += capacity
    wanted = lax.broadcasted_iota(jnp.int32, tags.shape, 1)
    wanted = ((wanted & 31) << 2) + (wanted >> 5) + 1
    hot[...] = jnp.where(tags[...] == wanted.astype(jnp.float32), 1.0, 0.0).T.astype(jnp.bfloat16)
    pick_rows(hot, xs, part, out_ref, 0)


def second_half_kernel(xs, hot, out_ref, part):
    pick_rows(hot, xs, part, out_ref, 1)


def sum_slots(arrived, capacity):
    rows = sum(x.shape[0] for x in arrived) // message_rows(capacity) * capacity
    vmem = pl.BlockSpec(memory_space=pltpu.VMEM)
    half = jax.ShapeDtypeStruct((SUB * 32, LANES), jnp.float32)
    params = pltpu.CompilerParams(vmem_limit_bytes=VMEM_LIMIT)
    part = pltpu.VMEM((SLOTS, LANES), jnp.float32)
    first, xs, hot = pl.pallas_call(
        functools.partial(first_half_kernel, capacity),
        out_shape=[
            half,
            jax.ShapeDtypeStruct((PIECES, rows, LANES), jnp.bfloat16),
            jax.ShapeDtypeStruct((SLOTS, rows), jnp.bfloat16),
        ],
        in_specs=[vmem] * len(arrived),
        out_specs=[vmem] * 3,
        scratch_shapes=[pltpu.VMEM((rows, LANES), jnp.float32), part],
        compiler_params=params,
        name="sum_first",
    )(*arrived)
    second = pl.pallas_call(
        second_half_kernel,
        out_shape=half,
        in_specs=[vmem] * 2,
        out_specs=vmem,
        scratch_shapes=[part],
        compiler_params=params,
        name="sum_second",
    )(xs, hot)
    return first, second


def add_kernel(at, mine_ref, theirs_ref, *refs):
    out_ref, total, sems = refs[-3:]
    step = total.shape[0] // sems.shape[0]
    copies = []
    for k in range(sems.shape[0]):
        here = pl.ds(k * step, step)
        total[here, :] = mine_ref[here, :] + theirs_ref[here, :]
        copy = pltpu.make_async_copy(
            total.at[here], out_ref.at[pl.ds(at + k * step, step)], sems.at[k]
        )
        copy.start()
        copies.append(copy)
    for copy in copies:
        copy.wait()


def add_half(at, mine, theirs, *whole):
    vmem, anywhere = pl.BlockSpec(memory_space=pltpu.VMEM), pl.BlockSpec(memory_space=pl.ANY)
    return pl.pallas_call(
        functools.partial(add_kernel, at),
        out_shape=jax.ShapeDtypeStruct((2 * mine.shape[0], LANES), jnp.float32),
        in_specs=[vmem, vmem] + [anywhere] * len(whole),
        out_specs=anywhere,
        scratch_shapes=[pltpu.VMEM(mine.shape, jnp.float32), pltpu.SemaphoreType.DMA((4,))],
        input_output_aliases={2: 0} if whole else {},
        compiler_params=pltpu.CompilerParams(vmem_limit_bytes=VMEM_LIMIT),
        name="add_half",
    )(mine, theirs, *whole)


def rows_of(array):
    blocks, parts, vis = array.shape
    tiles = vis // LANES
    split = array.reshape(blocks, parts, tiles, LANES)
    return split.transpose(0, 2, 1, 3).reshape(blocks * tiles * parts, LANES)


def sending_order(owners):
    across, near = list(range(max(owners // 2, 1), owners)), list(range(1, owners // 2))
    order = [across.pop() for _ in range(owners // 4)]
    while across or near:
        order += [group.pop() for group in (across, near) if group]
    return order + [0]


def in_rows(array):
    return with_layout_constraint(array, Layout(major_to_minor=(0, 1)))


def local(residual, uv_offsets, counts, tile_of_block, slot_of_block, owner_map):
    blocks, _, vis = uv_offsets.shape
    owners = owner_map.shape[0]
    capacity = -(-max(CAP_MIN, 2 * blocks // owners) // 32) * 16
    core = lax.axis_index("samp")
    me = lax.axis_index(("blk", "tile"))
    swap = [(0, 1), (1, 0)]
    own = in_rows(rows_of(residual[0]))
    other = in_rows(lax.ppermute(own, "samp", swap))

    lists = jnp.concatenate([tile_of_block[:, 0], slot_of_block, counts, owner_map])
    lists = lax.optimization_barrier(lists)
    tile_ids, slots, counts, owner_map = [
        lists[k * blocks : min((k + 1) * blocks, 3 * blocks + owners)] for k in range(4)
    ]
    owner_range = jnp.arange(owners, dtype=jnp.int32)
    owner_ids = jnp.sum(
        jnp.where(tile_ids[:, None] == owner_range[None, :], owner_map[None, :], 0), 1
    )
    paired = owners <= PAIRED_MAX and owners & (owners - 1) == 0
    distances = sending_order(owners)
    offset = owner_ids
    if paired:
        offset = jnp.bitwise_xor(owner_ids, me)
        offset = sum(jnp.where(offset == d, k, 0) for k, d in enumerate(distances) if k)
    index = jnp.arange(blocks, dtype=jnp.int32)
    same = (offset[None, :] == offset[:, None]) & (index[None, :] < index[:, None])
    rank = jnp.sum(same.astype(jnp.int32), 1)
    mine = (rank & 1) == core
    counted = jnp.sum((mine[None, :] & (offset[None, :] == owner_range[:, None])).astype(jnp.int32), 1)
    quads = (counted + QUAD - 1) >> 2
    edges = jnp.arange(owners + 1, dtype=jnp.int32)
    start = jnp.sum(jnp.where(owner_range[None, :] < edges[:, None], quads[None, :], 0), 1)
    before = jnp.sum(jnp.where(owner_range[None, :] < offset[:, None], quads[None, :], 0), 1)
    place = jnp.where(mine, before * QUAD + (rank >> 1), -1)
    longest = ((blocks + owners) // 2 + owners * (QUAD - 1)) // GROUP * GROUP + GROUP
    wanted = jnp.arange(longest, dtype=jnp.int32)
    chosen = place[None, :] == wanted[:, None]
    block_and_count = (index << COUNT_BITS) + counts
    row_and_tag = ((offset * capacity + (rank >> 1)) << TAG_BITS) + slots + 1
    block = jnp.sum(jnp.where(chosen, block_and_count[None, :], 0), 1)
    row = jnp.sum(jnp.where(chosen, row_and_tag[None, :], 0), 1)

    subgrids = functools.partial(
        make_subgrids, capacity=capacity, listed=longest, plan=jnp.concatenate([block, row, start]),
        uv=rows_of(uv_offsets), res=own.astype(jnp.float32) + other.astype(jnp.float32), vis=vis,
    )
    token = jnp.zeros((GROUP, LANES), jnp.int32)
    if paired:
        rows = []
        for first, last in zip(CALLS[:-1], CALLS[1:]):
            first, last = owners * first // CALLS[-1], owners * last // CALLS[-1]
            if first < last:
                *more, token = subgrids(first, (1,) * (last - first), token)
                rows += more
        arrived = []
        for distance, piece in zip(distances, rows):
            if distance:
                pairs = [(k, k ^ distance) for k in range(owners)]
                piece = lax.ppermute(piece, ("blk", "tile"), pairs)
            arrived.append(piece)
    else:
        each = max(d for d in range(1, 17) if owners % d == 0)
        rows = [subgrids(k, (each,), token)[0] for k in range(0, owners, each)]
        rows = jnp.concatenate(rows, 0).reshape(owners, message_rows(capacity), LANES)
        rows = lax.all_to_all(rows, ("blk", "tile"), split_axis=0, concat_axis=0, tiled=True)
        arrived = [rows.reshape(owners * message_rows(capacity), LANES)]
    first, second = sum_slots(arrived, capacity)
    whole = add_half(0, first, lax.ppermute(first, "samp", swap))
    whole = add_half(first.shape[0], second, lax.ppermute(second, "samp", swap), whole)
    whole = whole.reshape(SUB, SLOTS // 4, 2, LANES).transpose(0, 2, 1, 3)
    return whole.reshape(SUB, 2, SLOTS * SUB)


def solution(mesh):
    in_specs = (
        P("samp", ("cuts", "blk", "tile"), None, None),
        P(("cuts", "blk", "tile"), None, None),
        P(("cuts", "blk", "tile")),
        P(("cuts", "blk", "tile"), None),
        P(("cuts", "blk", "tile")),
        P(),
    )
    out_specs = P(("cuts", "blk", "tile"), None, None)
    return jax.shard_map(local, mesh=mesh, in_specs=in_specs, out_specs=out_specs, check_vma=False)
```

profile of v0, /device:TPU:0, one launch (start us, length us, event | category | flops | bytes accessed | tf_op | source)
XLA Modules:
  0.0 40.9 jit_solution(8219245536805467942)
XLA Ops:
  0.0 0.5 %collective-permute-start = (bf16[2048,128]{1,0:T(8,128)(2,1)}, bf16[2048,128]{1,0:T(8,128)(2,1)S(1)}, u32[]{:S(2)}, u32[]{:S(2)}) collective-permute-start(bf16[2048,128]{1,0:T(8,128)(2,1)} %bitcast.20), channel_id=1, source_target_pairs={{0,8},{8,0},{1,9},{9,1},{2,10},{10,2},{3,11},{11,3},{4,12},{12,4},... | collective-permute-start | bytes 1572872 | tf_op jit(solution)/shard_map/ppermute | solution.py:412
  0.5 0.0 copy-start.2
  0.5 0.0 copy-start.3
  0.5 0.0 copy-start.1
  0.5 0.0 copy-start.4
  0.5 0.7 %copy-done.2 = s32[256]{0:T(256)S(1)} copy-done((s32[256]{0:T(256)S(1)}, s32[256]{0:T(256)}, u32[]{:S(2)}) %copy-start.2) | copy-done | bytes 1048
  1.1 0.0 copy-done.3
  1.1 0.0 copy-done.1
  1.2 0.0 copy-done.4
  1.2 0.1 select_reduce_fusion.3
  1.3 0.2 convert_reduce_fusion
  1.5 0.1 convert_reduce_fusion.1
  1.6 0.1 select_reduce_fusion.2
  1.7 0.1 select_reduce_fusion.4
  1.8 0.2 select_reduce_fusion.1
  2.0 0.1 pad_add_fusion.1.plan_ref
  2.1 0.0 copy-start
  2.1 0.1 collective-permute-done
  2.2 1.2 %convert_add_fusion.res_ref = f32[2048,128]{1,0:T(8,128)S(1)} fusion(bf16[2048,128]{1,0:T(8,128)(2,1)S(1)} %collective-permute-done, bf16[2048,128]{1,0:T(8,128)(2,1)} %bitcast.21), kind=kLoop, calls=%fused_computation | loop fusion | flops 786432 | bytes 2097152 | tf_op jit(solution)/shard_map/add | solution.py:449
  3.4 0.0 copy-done
  3.4 4.0 %subgrids.4 = (bf16[528,128]{1,0:T(8,128)(2,1)S(1)}, bf16[528,128]{1,0:T(8,128)(2,1)S(1)}, s32[8,128]{1,0:T(8,128)S(1)}) custom-call(s32[329]{0:T(512)S(1)} %pad_add_fusion.1.plan_ref, s32[8,128]{1,0:T(8,128)S(1)} %broadcast_in_dim.112.token_ref, f32[2048,128]{1,0:T(8,128)S(1)} %bitcast.16, f32[2048,128]{1,0:T(8,128)S(1)} %convert_add_fusion.res_ref), custom_call_target="tpu_custom_call" | custom-call | flops 268435456 | bytes 524288 | tf_op jit(solution)/shard_map/subgrids/pallas_call | solution.py:256
  7.5 4.9 %collective-permute-start.1 = (bf16[528,128]{1,0:T(8,128)(2,1)S(1)}, bf16[528,128]{1,0:T(8,128)(2,1)S(1)}, u32[]{:S(2)}, u32[]{:S(2)}) collective-permute-start(bf16[528,128]{1,0:T(8,128)(2,1)S(1)} %get-tuple-element.19), channel_id=1, source_target_pairs={{0,7},{1,6},{2,5},{3,4},{4,3},{5,2},{6,1},{7,0},{8,15},{9,14},{10,... | collective-permute-start | bytes 405512 | tf_op jit(solution)/shard_map/ppermute | solution.py:463
  12.3 1.2 %collective-permute-start.2 = (bf16[528,128]{1,0:T(8,128)(2,1)S(1)}, bf16[528,128]{1,0:T(8,128)(2,1)S(1)}, u32[]{:S(2)}, u32[]{:S(2)}) collective-permute-start(bf16[528,128]{1,0:T(8,128)(2,1)S(1)} %get-tuple-element.20), channel_id=1, source_target_pairs={{0,6},{1,7},{2,4},{3,5},{4,2},{5,3},{6,0},{7,1},{8,14},{9,15},{10,... | collective-permute-start | bytes 405512 | tf_op jit(solution)/shard_map/ppermute | solution.py:463
  13.6 4.0 %subgrids.5 = (bf16[528,128]{1,0:T(8,128)(2,1)S(1)}, bf16[528,128]{1,0:T(8,128)(2,1)S(1)}, bf16[528,128]{1,0:T(8,128)(2,1)S(1)}, s32[8,128]{1,0:T(8,128)S(1)}) custom-call(s32[329]{0:T(512)S(1)} %pad_add_fusion.1.plan_ref, s32[8,128]{1,0:T(8,128)S(1)} %get-tuple-element.21.token_ref, f32[2048,128]{1,0:T(8,128)S(1)} %bitcast.17, ...), custom_call_target="tpu_custom_call" | custom-call | flops 402653184 | bytes 786432 | tf_op jit(solution)/shard_map/subgrids/pallas_call | solution.py:256
  17.6 0.1 collective-permute-start.3
  17.7 5.1 %collective-permute-start.4 = (bf16[528,128]{1,0:T(8,128)(2,1)S(1)}, bf16[528,128]{1,0:T(8,128)(2,1)S(1)}, u32[]{:S(2)}, u32[]{:S(2)}) collective-permute-start(bf16[528,128]{1,0:T(8,128)(2,1)S(1)} %get-tuple-element.23), channel_id=1, source_target_pairs={{0,3},{1,2},{2,1},{3,0},{4,7},{5,6},{6,5},{7,4},{8,11},{9,10},{10,... | collective-permute-start | bytes 405512 | tf_op jit(solution)/shard_map/ppermute | solution.py:463
  22.7 0.0 collective-permute-start.5
  22.7 3.5 %subgrids.6 = (bf16[528,128]{1,0:T(8,128)(2,1)S(1)}, bf16[528,128]{1,0:T(8,128)(2,1)S(1)}, s32[8,128]{1,0:T(8,128)S(1)}) custom-call(s32[329]{0:T(512)S(1)} %pad_add_fusion.1.plan_ref, s32[8,128]{1,0:T(8,128)S(1)} %get-tuple-element.25.token_ref, f32[2048,128]{1,0:T(8,128)S(1)} %bitcast.18, f32[2048,128]{1,0:T(8,128)S(1)} %convert_add_fusion.res_ref), custom_call_target="tpu_custom_call" | custom-call | flops 268435456 | bytes 524288 | tf_op jit(solution)/shard_map/subgrids/pallas_call | solution.py:256
  26.2 0.0 collective-permute-done.1.refs_0_
  26.3 0.5 %collective-permute-start.6 = (bf16[528,128]{1,0:T(8,128)(2,1)S(1)}, bf16[528,128]{1,0:T(8,128)(2,1)S(1)}, u32[]{:S(2)}, u32[]{:S(2)}) collective-permute-start(bf16[528,128]{1,0:T(8,128)(2,1)S(1)} %get-tuple-element.26), channel_id=1, source_target_pairs={{0,2},{1,3},{2,0},{3,1},{4,6},{5,7},{6,4},{7,5},{8,10},{9,11},{10,... | collective-permute-start | bytes 405512 | tf_op jit(solution)/shard_map/ppermute | solution.py:463
  26.8 0.0 collective-permute-done.2.refs_1_
  26.8 1.3 %collective-permute-start.7 = (bf16[528,128]{1,0:T(8,128)(2,1)S(1)}, bf16[528,128]{1,0:T(8,128)(2,1)S(1)}, u32[]{:S(2)}, u32[]{:S(2)}) collective-permute-start(bf16[528,128]{1,0:T(8,128)(2,1)S(1)} %get-tuple-element.27), channel_id=1, source_target_pairs={{0,1},{1,0},{2,3},{3,2},{4,5},{5,4},{6,7},{7,6},{8,9},{9,8},{10,11... | collective-permute-start | bytes 405512 | tf_op jit(solution)/shard_map/ppermute | solution.py:463
  28.0 1.9 %subgrids.7 = (bf16[528,128]{1,0:T(8,128)(2,1)S(1)}, s32[8,128]{1,0:T(8,128)}) custom-call(s32[329]{0:T(512)S(1)} %pad_add_fusion.1.plan_ref, s32[8,128]{1,0:T(8,128)S(1)} %get-tuple-element.28.token_ref, f32[2048,128]{1,0:T(8,128)S(1)} %bitcast.19, f32[2048,128]{1,0:T(8,128)S(1)} %convert_add_fusion.res_ref), custom_call_target="tpu_custom_call" | custom-call | flops 134217728 | bytes 262144 | tf_op jit(solution)/shard_map/subgrids/pallas_call | solution.py:256
  29.9 4.1 %collective-permute-done.3.refs_2_ = bf16[528,128]{1,0:T(8,128)(2,1)S(1)} collective-permute-done((bf16[528,128]{1,0:T(8,128)(2,1)S(1)}, bf16[528,128]{1,0:T(8,128)(2,1)S(1)}, u32[]{:S(2)}, u32[]{:S(2)}) %collective-permute-start.3) | collective-permute-done | bytes 135200 | tf_op jit(solution)/shard_map/ppermute | solution.py:463
  34.1 0.0 collective-permute-done.4.refs_3_
  34.1 2.3 %collective-permute-done.5.refs_4_ = bf16[528,128]{1,0:T(8,128)(2,1)S(1)} collective-permute-done((bf16[528,128]{1,0:T(8,128)(2,1)S(1)}, bf16[528,128]{1,0:T(8,128)(2,1)S(1)}, u32[]{:S(2)}, u32[]{:S(2)}) %collective-permute-start.5) | collective-permute-done | bytes 135200 | tf_op jit(solution)/shard_map/ppermute | solution.py:463
  36.3 0.1 collective-permute-done.6.refs_5_
  36.4 0.0 collective-permute-done.7.refs_6_
  36.4 0.8 %sum_first.1 = (f32[1024,128]{1,0:T(8,128)S(1)}, bf16[16,256,128]{2,1,0:T(8,128)(2,1)S(1)}, bf16[128,256]{1,0:T(8,128)(2,1)S(1)}) custom-call(bf16[528,128]{1,0:T(8,128)(2,1)S(1)} %collective-permute-done.1.refs_0_, bf16[528,128]{1,0:T(8,128)(2,1)S(1)} %collective-permute-done.2.refs_1_, bf16[528,128]{1,0:T(8,128)(2,1)S(1)} %collective-permute-done.3.refs_2_, ...), custom_call_target="tpu_custom_call" | custom-call | tf_op jit(solution)/shard_map/sum_first/pallas_call | solution.py:330
  37.2 0.1 collective-permute-start.9
  37.3 0.6 %sum_second.1.mine_ref = f32[1024,128]{1,0:T(8,128)S(1)} custom-call(bf16[16,256,128]{2,1,0:T(8,128)(2,1)S(1)} %get-tuple-element.30.xs, bf16[128,256]{1,0:T(8,128)(2,1)S(1)} %get-tuple-element.31.hot), custom_call_target="tpu_custom_call" | custom-call | tf_op jit(solution)/shard_map/sum_second/pallas_call | solution.py:343
  37.9 0.6 %collective-permute-start.8 = (f32[1024,128]{1,0:T(8,128)S(1)}, f32[1024,128]{1,0:T(8,128)S(1)}, u32[]{:S(2)}, u32[]{:S(2)}) collective-permute-start(f32[1024,128]{1,0:T(8,128)S(1)} %sum_second.1.mine_ref), channel_id=1, source_target_pairs={{0,8},{8,0},{1,9},{9,1},{2,10},{10,2},{3,11},{11,3},{4,12},{12,4},... | collective-permute-start | bytes 1572872 | tf_op jit(solution)/shard_map/ppermute | solution.py:473
  38.5 0.7 %collective-permute-done.9.theirs_ref = f32[1024,128]{1,0:T(8,128)S(1)} collective-permute-done((f32[1024,128]{1,0:T(8,128)S(1)}, f32[1024,128]{1,0:T(8,128)S(1)}, u32[]{:S(2)}, u32[]{:S(2)}) %collective-permute-start.9) | collective-permute-done | bytes 524320 | tf_op jit(solution)/shard_map/ppermute | solution.py:472
  39.2 0.8 %add_half.2.refs_0_ = f32[2048,128]{1,0:T(8,128)} custom-call(f32[1024,128]{1,0:T(8,128)S(1)} %get-tuple-element.32.mine_ref, f32[1024,128]{1,0:T(8,128)S(1)} %collective-permute-done.9.theirs_ref), custom_call_target="tpu_custom_call" | custom-call | tf_op jit(solution)/shard_map/add_half/pallas_call | solution.py:373
  40.0 0.0 collective-permute-done.8.theirs_ref
  40.1 0.8 %add_half.3 = f32[2048,128]{1,0:T(8,128)} custom-call(f32[1024,128]{1,0:T(8,128)S(1)} %sum_second.1.mine_ref, f32[1024,128]{1,0:T(8,128)S(1)} %collective-permute-done.8.theirs_ref, f32[2048,128]{1,0:T(8,128)} %add_half.2.refs_0_), custom_call_target="tpu_custom_call", output_to_operand_aliasing={{}: (2, {})} | custom-call | tf_op jit(solution)/shard_map/add_half/pallas_call | solution.py:373
  (8 shorter events, 0.1 us)
Async XLA Ops:
  0.0 2.2 %collective-permute-start = (bf16[2048,128]{1,0:T(8,128)(2,1)}, bf16[2048,128]{1,0:T(8,128)(2,1)S(1)}, u32[]{:S(2)}, u32[]{:S(2)}) collective-permute-start(bf16[2048,128]{1,0:T(8,128)(2,1)} %bitcast.20), channel_id=1, source_target_pairs={{0,8},{8,0},{1,9},{9,1},{2,10},{10,2},{3,11},{11,3},{4,12},{12,4},... | collective-permute-start | bytes 1572872 | tf_op jit(solution)/shard_map/ppermute | solution.py:412
  0.5 0.7 %copy-start.2 = (s32[256]{0:T(256)S(1)}, s32[256]{0:T(256)}, u32[]{:S(2)}) copy-start(s32[256]{0:T(256)} %param.10) | copy-start | bytes 3076
  0.5 0.7 %copy-start.3 = (s32[256,1]{0,1:T(1,128)S(1)}, s32[256,1]{0,1:T(1,128)}, u32[]{:S(2)}) copy-start(s32[256,1]{0,1:T(1,128)} %param.9) | copy-start | bytes 3076
  0.5 0.7 %copy-start.1 = (s32[256]{0:T(256)S(1)}, s32[256]{0:T(256)}, u32[]{:S(2)}) copy-start(s32[256]{0:T(256)} %param.8) | copy-start | bytes 3076
  0.5 0.7 %copy-start.4 = (s32[8]{0:T(128)S(1)}, s32[8]{0:T(128)}, u32[]{:S(2)}) copy-start(s32[8]{0:T(128)} %param.11) | copy-start | bytes 100
  2.1 1.4 %copy-start = (f32[256,2,512]{2,1,0:T(2,128)S(1)}, f32[256,2,512]{2,1,0:T(2,128)}, u32[]{:S(2)}) copy-start(f32[256,2,512]{2,1,0:T(2,128)} %param.7) | copy-start | bytes 3145732
  7.5 18.8 %collective-permute-start.1 = (bf16[528,128]{1,0:T(8,128)(2,1)S(1)}, bf16[528,128]{1,0:T(8,128)(2,1)S(1)}, u32[]{:S(2)}, u32[]{:S(2)}) collective-permute-start(bf16[528,128]{1,0:T(8,128)(2,1)S(1)} %get-tuple-element.19), channel_id=1, source_target_pairs={{0,7},{1,6},{2,5},{3,4},{4,3},{5,2},{6,1},{7,0},{8,15},{9,14},{10,... | collective-permute-start | bytes 405512 | tf_op jit(solution)/shard_map/ppermute | solution.py:463
  12.3 14.5 %collective-permute-start.2 = (bf16[528,128]{1,0:T(8,128)(2,1)S(1)}, bf16[528,128]{1,0:T(8,128)(2,1)S(1)}, u32[]{:S(2)}, u32[]{:S(2)}) collective-permute-start(bf16[528,128]{1,0:T(8,128)(2,1)S(1)} %get-tuple-element.20), channel_id=1, source_target_pairs={{0,6},{1,7},{2,4},{3,5},{4,2},{5,3},{6,0},{7,1},{8,14},{9,15},{10,... | collective-permute-start | bytes 405512 | tf_op jit(solution)/shard_map/ppermute | solution.py:463
  17.6 16.5 %collective-permute-start.3 = (bf16[528,128]{1,0:T(8,128)(2,1)S(1)}, bf16[528,128]{1,0:T(8,128)(2,1)S(1)}, u32[]{:S(2)}, u32[]{:S(2)}) collective-permute-start(bf16[528,128]{1,0:T(8,128)(2,1)S(1)} %get-tuple-element.22), channel_id=1, source_target_pairs={{0,5},{1,4},{2,7},{3,6},{4,1},{5,0},{6,3},{7,2},{8,13},{9,12},{10,... | collective-permute-start | bytes 405512 | tf_op jit(solution)/shard_map/ppermute | solution.py:463
  17.7 16.4 %collective-permute-start.4 = (bf16[528,128]{1,0:T(8,128)(2,1)S(1)}, bf16[528,128]{1,0:T(8,128)(2,1)S(1)}, u32[]{:S(2)}, u32[]{:S(2)}) collective-permute-start(bf16[528,128]{1,0:T(8,128)(2,1)S(1)} %get-tuple-element.23), channel_id=1, source_target_pairs={{0,3},{1,2},{2,1},{3,0},{4,7},{5,6},{6,5},{7,4},{8,11},{9,10},{10,... | collective-permute-start | bytes 405512 | tf_op jit(solution)/shard_map/ppermute | solution.py:463
  22.7 13.6 %collective-permute-start.5 = (bf16[528,128]{1,0:T(8,128)(2,1)S(1)}, bf16[528,128]{1,0:T(8,128)(2,1)S(1)}, u32[]{:S(2)}, u32[]{:S(2)}) collective-permute-start(bf16[528,128]{1,0:T(8,128)(2,1)S(1)} %get-tuple-element.24), channel_id=1, source_target_pairs={{0,4},{1,5},{2,6},{3,7},{4,0},{5,1},{6,2},{7,3},{8,12},{9,13},{10,... | collective-permute-start | bytes 405512 | tf_op jit(solution)/shard_map/ppermute | solution.py:463
  26.3 10.1 %collective-permute-start.6 = (bf16[528,128]{1,0:T(8,128)(2,1)S(1)}, bf16[528,128]{1,0:T(8,128)(2,1)S(1)}, u32[]{:S(2)}, u32[]{:S(2)}) collective-permute-start(bf16[528,128]{1,0:T(8,128)(2,1)S(1)} %get-tuple-element.26), channel_id=1, source_target_pairs={{0,2},{1,3},{2,0},{3,1},{4,6},{5,7},{6,4},{7,5},{8,10},{9,11},{10,... | collective-permute-start | bytes 405512 | tf_op jit(solution)/shard_map/ppermute | solution.py:463
  26.8 9.6 %collective-permute-start.7 = (bf16[528,128]{1,0:T(8,128)(2,1)S(1)}, bf16[528,128]{1,0:T(8,128)(2,1)S(1)}, u32[]{:S(2)}, u32[]{:S(2)}) collective-permute-start(bf16[528,128]{1,0:T(8,128)(2,1)S(1)} %get-tuple-element.27), channel_id=1, source_target_pairs={{0,1},{1,0},{2,3},{3,2},{4,5},{5,4},{6,7},{7,6},{8,9},{9,8},{10,11... | collective-permute-start | bytes 405512 | tf_op jit(solution)/shard_map/ppermute | solution.py:463
  37.2 2.0 %collective-permute-start.9 = (f32[1024,128]{1,0:T(8,128)S(1)}, f32[1024,128]{1,0:T(8,128)S(1)}, u32[]{:S(2)}, u32[]{:S(2)}) collective-permute-start(f32[1024,128]{1,0:T(8,128)S(1)} %get-tuple-element.32.mine_ref), channel_id=1, source_target_pairs={{0,8},{8,0},{1,9},{9,1},{2,10},{10,2},{3,11},{11,3},{4,12},{12,4},... | collective-permute-start | bytes 1572872 | tf_op jit(solution)/shard_map/ppermute | solution.py:472
  37.9 2.1 %collective-permute-start.8 = (f32[1024,128]{1,0:T(8,128)S(1)}, f32[1024,128]{1,0:T(8,128)S(1)}, u32[]{:S(2)}, u32[]{:S(2)}) collective-permute-start(f32[1024,128]{1,0:T(8,128)S(1)} %sum_second.1.mine_ref), channel_id=1, source_target_pairs={{0,8},{8,0},{1,9},{9,1},{2,10},{10,2},{3,11},{11,3},{4,12},{12,4},... | collective-permute-start | bytes 1572872 | tf_op jit(solution)/shard_map/ppermute | solution.py:473
where the time goes:
time: 40.9 us
  Pallas kernels  16.5 us (40%)
  starting transfers between devices  14.1 us (34%)
  waiting for transfers between devices  7.34 us (18%)
  other arithmetic  2.06 us (5%)
  local copies, waits for them, and re-layouts  0.73 us (2%)
    pallas_call x4, Pallas kernels, make_subgrids(): pl.pallas_call(functools.partial(subgrid_kernel, first, destinations, cap...  13.4 us
    ppermute x7, starting transfers between devices, local(): piece = lax.ppermute(piece, ('blk', 'tile'), pairs)  13 us
    ppermute x7, waiting for transfers between devices, local(): piece = lax.ppermute(piece, ('blk', 'tile'), pairs)  6.48 us
    pallas_call x2, Pallas kernels, add_half(): pl.pallas_call(functools.partial(add_kernel, at), out_shape=jax.ShapeDtyp...  1.67 us
    add x1, other arithmetic, local(): own.astype(jnp.float32) + other.astype(jnp.float32)  1.22 us
    pallas_call x1, Pallas kernels, sum_slots(): pl.pallas_call(functools.partial(first_half_kernel, capacity), out_shape=...  0.82 us
  transfers between devices with their start and end apart: 10, of which 5 were waited for; matrix products, arithmetic and copies ran while one was open for 2% of the time, Pallas kernels for 27%

commit v1 on v0

--- a/solution.py
+++ b/solution.py
@@ -23,7 +23,7 @@
 TAG_BITS = 8
 CHUNK = 4 * LANES
 PAIRED_MAX = 16
-CALLS = (0, 2, 5, 7, 8)
+CALLS = (0, 2, 4, 7, 8)
 VMEM_LIMIT = 48 * 1024 * 1024
 
 
@@ -390,11 +390,7 @@
 
 
 def sending_order(owners):
-    across, near = list(range(max(owners // 2, 1), owners)), list(range(1, owners // 2))
-    order = [across.pop() for _ in range(owners // 4)]
-    while across or near:
-        order += [group.pop() for group in (across, near) if group]
-    return order + [0]
+    return list(range(owners - 1, -1, -1))
 
 
 def in_rows(array):

time: 40.9 us -> 43.8 us (1.071); the launches traced: 40.9 us -> 43.3 us
  starting transfers between devices: 14.1 us -> 17.5 us
  waiting for transfers between devices: 7.34 us -> 5.84 us
  Pallas kernels: 16.5 us -> 17 us
    ppermute x7, starting transfers between devices: 13 us -> 16.4 us  [local(): piece = lax.ppermute(piece, ('blk', 'tile'), pairs)]
    ppermute x7, waiting for transfers between devices: 6.48 us -> 4.99 us  [local(): piece = lax.ppermute(piece, ('blk', 'tile'), pairs)]
    pallas_call x4, Pallas kernels: 13.4 us -> 13.9 us  [make_subgrids(): pl.pallas_call(functools.partial(subgrid_kernel, first, destinations, cap...]
  transfers between devices with their start and end apart: 10 -> 10, of which waited for: 5 -> 4; matrix products, arithmetic and copies ran while one was open for 2% -> 2% of each run, Pallas kernels for 27% -> 29%
where the time goes in v1:
time: 43.8 us; the launch traced here: 43.3 us
  starting transfers between devices  17.5 us (40%)
  Pallas kernels  17 us (39%)
  waiting for transfers between devices  5.84 us (13%)
  other arithmetic  2.06 us (5%)
  local copies, waits for them, and re-layouts  0.73 us (2%)
    ppermute x7, starting transfers between devices, local(): piece = lax.ppermute(piece, ('blk', 'tile'), pairs)  16.4 us
    pallas_call x4, Pallas kernels, make_subgrids(): pl.pallas_call(functools.partial(subgrid_kernel, first, destinations, cap...  13.9 us
    ppermute x7, waiting for transfers between devices, local(): piece = lax.ppermute(piece, ('blk', 'tile'), pairs)  4.99 us
    pallas_call x2, Pallas kernels, add_half(): pl.pallas_call(functools.partial(add_kernel, at), out_shape=jax.ShapeDtyp...  1.67 us
    add x1, other arithmetic, local(): own.astype(jnp.float32) + other.astype(jnp.float32)  1.22 us
  transfers between devices with their start and end apart: 10, of which 4 were waited for; matrix products, arithmetic and copies ran while one was open for 2% of the time, Pallas kernels for 29%

profile of v1, /device:TPU:0, one launch (start us, length us, event | category | flops | bytes accessed | tf_op | source)
XLA Modules:
  0.0 43.3 jit_solution(12847098101238494679)
XLA Ops:
  0.0 0.5 %collective-permute-start = (bf16[2048,128]{1,0:T(8,128)(2,1)}, bf16[2048,128]{1,0:T(8,128)(2,1)S(1)}, u32[]{:S(2)}, u32[]{:S(2)}) collective-permute-start(bf16[2048,128]{1,0:T(8,128)(2,1)} %bitcast.20), channel_id=1, source_target_pairs={{0,8},{8,0},{1,9},{9,1},{2,10},{10,2},{3,11},{11,3},{4,12},{12,4},... | collective-permute-start | bytes 1572872 | tf_op jit(solution)/shard_map/ppermute | solution.py:408
  0.5 0.0 copy-start.2
  0.5 0.0 copy-start.3
  0.5 0.0 copy-start.1
  0.5 0.0 copy-start.4
  0.5 0.7 %copy-done.2 = s32[256]{0:T(256)S(1)} copy-done((s32[256]{0:T(256)S(1)}, s32[256]{0:T(256)}, u32[]{:S(2)}) %copy-start.2) | copy-done | bytes 1048
  1.1 0.0 copy-done.3
  1.1 0.0 copy-done.1
  1.2 0.0 copy-done.4
  1.2 0.1 select_reduce_fusion.3
  1.3 0.2 convert_reduce_fusion
  1.5 0.1 convert_reduce_fusion.1
  1.6 0.1 select_reduce_fusion.2
  1.7 0.1 select_reduce_fusion.4
  1.8 0.2 select_reduce_fusion.1
  2.0 0.1 pad_add_fusion.1.plan_ref
  2.1 0.0 copy-start
  2.1 0.1 collective-permute-done
  2.2 1.2 %convert_add_fusion.res_ref = f32[2048,128]{1,0:T(8,128)S(1)} fusion(bf16[2048,128]{1,0:T(8,128)(2,1)S(1)} %collective-permute-done, bf16[2048,128]{1,0:T(8,128)(2,1)} %bitcast.21), kind=kLoop, calls=%fused_computation | loop fusion | flops 786432 | bytes 2097152 | tf_op jit(solution)/shard_map/add | solution.py:445
  3.4 0.0 copy-done
  3.4 3.0 %subgrids.4 = (bf16[528,128]{1,0:T(8,128)(2,1)S(1)}, bf16[528,128]{1,0:T(8,128)(2,1)S(1)}, s32[8,128]{1,0:T(8,128)S(1)}) custom-call(s32[329]{0:T(512)S(1)} %pad_add_fusion.1.plan_ref, s32[8,128]{1,0:T(8,128)S(1)} %broadcast_in_dim.115.token_ref, f32[2048,128]{1,0:T(8,128)S(1)} %bitcast.16, f32[2048,128]{1,0:T(8,128)S(1)} %convert_add_fusion.res_ref), custom_call_target="tpu_custom_call" | custom-call | flops 268435456 | bytes 524288 | tf_op jit(solution)/shard_map/subgrids/pallas_call | solution.py:256
  6.5 5.9 %collective-permute-start.1 = (bf16[528,128]{1,0:T(8,128)(2,1)S(1)}, bf16[528,128]{1,0:T(8,128)(2,1)S(1)}, u32[]{:S(2)}, u32[]{:S(2)}) collective-permute-start(bf16[528,128]{1,0:T(8,128)(2,1)S(1)} %get-tuple-element.19), channel_id=1, source_target_pairs={{0,7},{1,6},{2,5},{3,4},{4,3},{5,2},{6,1},{7,0},{8,15},{9,14},{10,... | collective-permute-start | bytes 405512 | tf_op jit(solution)/shard_map/ppermute | solution.py:459
  12.3 0.7 %collective-permute-start.2 = (bf16[528,128]{1,0:T(8,128)(2,1)S(1)}, bf16[528,128]{1,0:T(8,128)(2,1)S(1)}, u32[]{:S(2)}, u32[]{:S(2)}) collective-permute-start(bf16[528,128]{1,0:T(8,128)(2,1)S(1)} %get-tuple-element.20), channel_id=1, source_target_pairs={{0,6},{1,7},{2,4},{3,5},{4,2},{5,3},{6,0},{7,1},{8,14},{9,15},{10,... | collective-permute-start | bytes 405512 | tf_op jit(solution)/shard_map/ppermute | solution.py:459
  13.1 4.5 %subgrids.5 = (bf16[528,128]{1,0:T(8,128)(2,1)S(1)}, bf16[528,128]{1,0:T(8,128)(2,1)S(1)}, s32[8,128]{1,0:T(8,128)S(1)}) custom-call(s32[329]{0:T(512)S(1)} %pad_add_fusion.1.plan_ref, s32[8,128]{1,0:T(8,128)S(1)} %get-tuple-element.21.token_ref, f32[2048,128]{1,0:T(8,128)S(1)} %bitcast.17, f32[2048,128]{1,0:T(8,128)S(1)} %convert_add_fusion.res_ref), custom_call_target="tpu_custom_call" | custom-call | flops 268435456 | bytes 524288 | tf_op jit(solution)/shard_map/subgrids/pallas_call | solution.py:256
  17.6 0.1 collective-permute-start.3
  17.7 1.8 %collective-permute-start.4 = (bf16[528,128]{1,0:T(8,128)(2,1)S(1)}, bf16[528,128]{1,0:T(8,128)(2,1)S(1)}, u32[]{:S(2)}, u32[]{:S(2)}) collective-permute-start(bf16[528,128]{1,0:T(8,128)(2,1)S(1)} %get-tuple-element.23), channel_id=1, source_target_pairs={{0,4},{1,5},{2,6},{3,7},{4,0},{5,1},{6,2},{7,3},{8,12},{9,13},{10,... | collective-permute-start | bytes 405512 | tf_op jit(solution)/shard_map/ppermute | solution.py:459
  19.4 4.5 %subgrids.6 = (bf16[528,128]{1,0:T(8,128)(2,1)S(1)}, bf16[528,128]{1,0:T(8,128)(2,1)S(1)}, bf16[528,128]{1,0:T(8,128)(2,1)S(1)}, s32[8,128]{1,0:T(8,128)S(1)}) custom-call(s32[329]{0:T(512)S(1)} %pad_add_fusion.1.plan_ref, s32[8,128]{1,0:T(8,128)S(1)} %get-tuple-element.24.token_ref, f32[2048,128]{1,0:T(8,128)S(1)} %bitcast.18, ...), custom_call_target="tpu_custom_call" | custom-call | flops 402653184 | bytes 786432 | tf_op jit(solution)/shard_map/subgrids/pallas_call | solution.py:256
  24.0 0.8 %collective-permute-start.5 = (bf16[528,128]{1,0:T(8,128)(2,1)S(1)}, bf16[528,128]{1,0:T(8,128)(2,1)S(1)}, u32[]{:S(2)}, u32[]{:S(2)}) collective-permute-start(bf16[528,128]{1,0:T(8,128)(2,1)S(1)} %get-tuple-element.25), channel_id=1, source_target_pairs={{0,3},{1,2},{2,1},{3,0},{4,7},{5,6},{6,5},{7,4},{8,11},{9,10},{10,... | collective-permute-start | bytes 405512 | tf_op jit(solution)/shard_map/ppermute | solution.py:459
  24.8 0.0 collective-permute-done.1.refs_0_
  24.8 4.3 %collective-permute-start.6 = (bf16[528,128]{1,0:T(8,128)(2,1)S(1)}, bf16[528,128]{1,0:T(8,128)(2,1)S(1)}, u32[]{:S(2)}, u32[]{:S(2)}) collective-permute-start(bf16[528,128]{1,0:T(8,128)(2,1)S(1)} %get-tuple-element.26), channel_id=1, source_target_pairs={{0,2},{1,3},{2,0},{3,1},{4,6},{5,7},{6,4},{7,5},{8,10},{9,11},{10,... | collective-permute-start | bytes 405512 | tf_op jit(solution)/shard_map/ppermute | solution.py:459
  29.1 0.0 collective-permute-done.2.refs_1_
  29.1 2.8 %collective-permute-start.7 = (bf16[528,128]{1,0:T(8,128)(2,1)S(1)}, bf16[528,128]{1,0:T(8,128)(2,1)S(1)}, u32[]{:S(2)}, u32[]{:S(2)}) collective-permute-start(bf16[528,128]{1,0:T(8,128)(2,1)S(1)} %get-tuple-element.27), channel_id=1, source_target_pairs={{0,1},{1,0},{2,3},{3,2},{4,5},{5,4},{6,7},{7,6},{8,9},{9,8},{10,11... | collective-permute-start | bytes 405512 | tf_op jit(solution)/shard_map/ppermute | solution.py:459
  31.9 1.9 %subgrids.7 = (bf16[528,128]{1,0:T(8,128)(2,1)S(1)}, s32[8,128]{1,0:T(8,128)}) custom-call(s32[329]{0:T(512)S(1)} %pad_add_fusion.1.plan_ref, s32[8,128]{1,0:T(8,128)S(1)} %get-tuple-element.28.token_ref, f32[2048,128]{1,0:T(8,128)S(1)} %bitcast.19, f32[2048,128]{1,0:T(8,128)S(1)} %convert_add_fusion.res_ref), custom_call_target="tpu_custom_call" | custom-call | flops 134217728 | bytes 262144 | tf_op jit(solution)/shard_map/subgrids/pallas_call | solution.py:256
  33.8 0.0 collective-permute-done.3.refs_2_
  33.8 3.5 %collective-permute-done.4.refs_3_ = bf16[528,128]{1,0:T(8,128)(2,1)S(1)} collective-permute-done((bf16[528,128]{1,0:T(8,128)(2,1)S(1)}, bf16[528,128]{1,0:T(8,128)(2,1)S(1)}, u32[]{:S(2)}, u32[]{:S(2)}) %collective-permute-start.4) | collective-permute-done | bytes 135200 | tf_op jit(solution)/shard_map/ppermute | solution.py:459
  37.4 0.0 collective-permute-done.5.refs_4_
  37.4 1.4 %collective-permute-done.6.refs_5_ = bf16[528,128]{1,0:T(8,128)(2,1)S(1)} collective-permute-done((bf16[528,128]{1,0:T(8,128)(2,1)S(1)}, bf16[528,128]{1,0:T(8,128)(2,1)S(1)}, u32[]{:S(2)}, u32[]{:S(2)}) %collective-permute-start.6) | collective-permute-done | bytes 135200 | tf_op jit(solution)/shard_map/ppermute | solution.py:459
  38.8 0.0 collective-permute-done.7.refs_6_
  38.8 0.8 %sum_first.1 = (f32[1024,128]{1,0:T(8,128)S(1)}, bf16[16,256,128]{2,1,0:T(8,128)(2,1)S(1)}, bf16[128,256]{1,0:T(8,128)(2,1)S(1)}) custom-call(bf16[528,128]{1,0:T(8,128)(2,1)S(1)} %collective-permute-done.1.refs_0_, bf16[528,128]{1,0:T(8,128)(2,1)S(1)} %collective-permute-done.2.refs_1_, bf16[528,128]{1,0:T(8,128)(2,1)S(1)} %collective-permute-done.3.refs_2_, ...), custom_call_target="tpu_custom_call" | custom-call | tf_op jit(solution)/shard_map/sum_first/pallas_call | solution.py:330
  39.6 0.1 collective-permute-start.9
  39.7 0.6 %sum_second.1.mine_ref = f32[1024,128]{1,0:T(8,128)S(1)} custom-call(bf16[16,256,128]{2,1,0:T(8,128)(2,1)S(1)} %get-tuple-element.30.xs, bf16[128,256]{1,0:T(8,128)(2,1)S(1)} %get-tuple-element.31.hot), custom_call_target="tpu_custom_call" | custom-call | tf_op jit(solution)/shard_map/sum_second/pallas_call | solution.py:343
  40.3 0.6 %collective-permute-start.8 = (f32[1024,128]{1,0:T(8,128)S(1)}, f32[1024,128]{1,0:T(8,128)S(1)}, u32[]{:S(2)}, u32[]{:S(2)}) collective-permute-start(f32[1024,128]{1,0:T(8,128)S(1)} %sum_second.1.mine_ref), channel_id=1, source_target_pairs={{0,8},{8,0},{1,9},{9,1},{2,10},{10,2},{3,11},{11,3},{4,12},{12,4},... | collective-permute-start | bytes 1572872 | tf_op jit(solution)/shard_map/ppermute | solution.py:469
  40.9 0.7 %collective-permute-done.9.theirs_ref = f32[1024,128]{1,0:T(8,128)S(1)} collective-permute-done((f32[1024,128]{1,0:T(8,128)S(1)}, f32[1024,128]{1,0:T(8,128)S(1)}, u32[]{:S(2)}, u32[]{:S(2)}) %collective-permute-start.9) | collective-permute-done | bytes 524320 | tf_op jit(solution)/shard_map/ppermute | solution.py:468
  41.6 0.8 %add_half.2.refs_0_ = f32[2048,128]{1,0:T(8,128)} custom-call(f32[1024,128]{1,0:T(8,128)S(1)} %get-tuple-element.32.mine_ref, f32[1024,128]{1,0:T(8,128)S(1)} %collective-permute-done.9.theirs_ref), custom_call_target="tpu_custom_call" | custom-call | tf_op jit(solution)/shard_map/add_half/pallas_call | solution.py:373
  42.4 0.0 collective-permute-done.8.theirs_ref
  42.4 0.8 %add_half.3 = f32[2048,128]{1,0:T(8,128)} custom-call(f32[1024,128]{1,0:T(8,128)S(1)} %sum_second.1.mine_ref, f32[1024,128]{1,0:T(8,128)S(1)} %collective-permute-done.8.theirs_ref, f32[2048,128]{1,0:T(8,128)} %add_half.2.refs_0_), custom_call_target="tpu_custom_call", output_to_operand_aliasing={{}: (2, {})} | custom-call | tf_op jit(solution)/shard_map/add_half/pallas_call | solution.py:373
  (8 shorter events, 0.1 us)
Async XLA Ops:
  0.0 2.2 %collective-permute-start = (bf16[2048,128]{1,0:T(8,128)(2,1)}, bf16[2048,128]{1,0:T(8,128)(2,1)S(1)}, u32[]{:S(2)}, u32[]{:S(2)}) collective-permute-start(bf16[2048,128]{1,0:T(8,128)(2,1)} %bitcast.20), channel_id=1, source_target_pairs={{0,8},{8,0},{1,9},{9,1},{2,10},{10,2},{3,11},{11,3},{4,12},{12,4},... | collective-permute-start | bytes 1572872 | tf_op jit(solution)/shard_map/ppermute | solution.py:408
  0.5 0.7 %copy-start.2 = (s32[256]{0:T(256)S(1)}, s32[256]{0:T(256)}, u32[]{:S(2)}) copy-start(s32[256]{0:T(256)} %param.10) | copy-start | bytes 3076
  0.5 0.7 %copy-start.3 = (s32[256,1]{0,1:T(1,128)S(1)}, s32[256,1]{0,1:T(1,128)}, u32[]{:S(2)}) copy-start(s32[256,1]{0,1:T(1,128)} %param.9) | copy-start | bytes 3076
  0.5 0.7 %copy-start.1 = (s32[256]{0:T(256)S(1)}, s32[256]{0:T(256)}, u32[]{:S(2)}) copy-start(s32[256]{0:T(256)} %param.8) | copy-start | bytes 3076
  0.5 0.7 %copy-start.4 = (s32[8]{0:T(128)S(1)}, s32[8]{0:T(128)}, u32[]{:S(2)}) copy-start(s32[8]{0:T(128)} %param.11) | copy-start | bytes 100
  2.1 1.4 %copy-start = (f32[256,2,512]{2,1,0:T(2,128)S(1)}, f32[256,2,512]{2,1,0:T(2,128)}, u32[]{:S(2)}) copy-start(f32[256,2,512]{2,1,0:T(2,128)} %param.7) | copy-start | bytes 3145732
  6.5 18.3 %collective-permute-start.1 = (bf16[528,128]{1,0:T(8,128)(2,1)S(1)}, bf16[528,128]{1,0:T(8,128)(2,1)S(1)}, u32[]{:S(2)}, u32[]{:S(2)}) collective-permute-start(bf16[528,128]{1,0:T(8,128)(2,1)S(1)} %get-tuple-element.19), channel_id=1, source_target_pairs={{0,7},{1,6},{2,5},{3,4},{4,3},{5,2},{6,1},{7,0},{8,15},{9,14},{10,... | collective-permute-start | bytes 405512 | tf_op jit(solution)/shard_map/ppermute | solution.py:459
  12.3 16.8 %collective-permute-start.2 = (bf16[528,128]{1,0:T(8,128)(2,1)S(1)}, bf16[528,128]{1,0:T(8,128)(2,1)S(1)}, u32[]{:S(2)}, u32[]{:S(2)}) collective-permute-start(bf16[528,128]{1,0:T(8,128)(2,1)S(1)} %get-tuple-element.20), channel_id=1, source_target_pairs={{0,6},{1,7},{2,4},{3,5},{4,2},{5,3},{6,0},{7,1},{8,14},{9,15},{10,... | collective-permute-start | bytes 405512 | tf_op jit(solution)/shard_map/ppermute | solution.py:459
  17.6 16.3 %collective-permute-start.3 = (bf16[528,128]{1,0:T(8,128)(2,1)S(1)}, bf16[528,128]{1,0:T(8,128)(2,1)S(1)}, u32[]{:S(2)}, u32[]{:S(2)}) collective-permute-start(bf16[528,128]{1,0:T(8,128)(2,1)S(1)} %get-tuple-element.22), channel_id=1, source_target_pairs={{0,5},{1,4},{2,7},{3,6},{4,1},{5,0},{6,3},{7,2},{8,13},{9,12},{10,... | collective-permute-start | bytes 405512 | tf_op jit(solution)/shard_map/ppermute | solution.py:459
  17.7 19.7 %collective-permute-start.4 = (bf16[528,128]{1,0:T(8,128)(2,1)S(1)}, bf16[528,128]{1,0:T(8,128)(2,1)S(1)}, u32[]{:S(2)}, u32[]{:S(2)}) collective-permute-start(bf16[528,128]{1,0:T(8,128)(2,1)S(1)} %get-tuple-element.23), channel_id=1, source_target_pairs={{0,4},{1,5},{2,6},{3,7},{4,0},{5,1},{6,2},{7,3},{8,12},{9,13},{10,... | collective-permute-start | bytes 405512 | tf_op jit(solution)/shard_map/ppermute | solution.py:459
  24.0 13.4 %collective-permute-start.5 = (bf16[528,128]{1,0:T(8,128)(2,1)S(1)}, bf16[528,128]{1,0:T(8,128)(2,1)S(1)}, u32[]{:S(2)}, u32[]{:S(2)}) collective-permute-start(bf16[528,128]{1,0:T(8,128)(2,1)S(1)} %get-tuple-element.25), channel_id=1, source_target_pairs={{0,3},{1,2},{2,1},{3,0},{4,7},{5,6},{6,5},{7,4},{8,11},{9,10},{10,... | collective-permute-start | bytes 405512 | tf_op jit(solution)/shard_map/ppermute | solution.py:459
  24.8 14.0 %collective-permute-start.6 = (bf16[528,128]{1,0:T(8,128)(2,1)S(1)}, bf16[528,128]{1,0:T(8,128)(2,1)S(1)}, u32[]{:S(2)}, u32[]{:S(2)}) collective-permute-start(bf16[528,128]{1,0:T(8,128)(2,1)S(1)} %get-tuple-element.26), channel_id=1, source_target_pairs={{0,2},{1,3},{2,0},{3,1},{4,6},{5,7},{6,4},{7,5},{8,10},{9,11},{10,... | collective-permute-start | bytes 405512 | tf_op jit(solution)/shard_map/ppermute | solution.py:459
  29.1 9.7 %collective-permute-start.7 = (bf16[528,128]{1,0:T(8,128)(2,1)S(1)}, bf16[528,128]{1,0:T(8,128)(2,1)S(1)}, u32[]{:S(2)}, u32[]{:S(2)}) collective-permute-start(bf16[528,128]{1,0:T(8,128)(2,1)S(1)} %get-tuple-element.27), channel_id=1, source_target_pairs={{0,1},{1,0},{2,3},{3,2},{4,5},{5,4},{6,7},{7,6},{8,9},{9,8},{10,11... | collective-permute-start | bytes 405512 | tf_op jit(solution)/shard_map/ppermute | solution.py:459
  39.6 2.0 %collective-permute-start.9 = (f32[1024,128]{1,0:T(8,128)S(1)}, f32[1024,128]{1,0:T(8,128)S(1)}, u32[]{:S(2)}, u32[]{:S(2)}) collective-permute-start(f32[1024,128]{1,0:T(8,128)S(1)} %get-tuple-element.32.mine_ref), channel_id=1, source_target_pairs={{0,8},{8,0},{1,9},{9,1},{2,10},{10,2},{3,11},{11,3},{4,12},{12,4},... | collective-permute-start | bytes 1572872 | tf_op jit(solution)/shard_map/ppermute | solution.py:468
  40.3 2.1 %collective-permute-start.8 = (f32[1024,128]{1,0:T(8,128)S(1)}, f32[1024,128]{1,0:T(8,128)S(1)}, u32[]{:S(2)}, u32[]{:S(2)}) collective-permute-start(f32[1024,128]{1,0:T(8,128)S(1)} %sum_second.1.mine_ref), channel_id=1, source_target_pairs={{0,8},{8,0},{1,9},{9,1},{2,10},{10,2},{3,11},{11,3},{4,12},{12,4},... | collective-permute-start | bytes 1572872 | tf_op jit(solution)/shard_map/ppermute | solution.py:469

commit v2 on v1

--- a/solution.py
+++ b/solution.py
@@ -23,7 +23,7 @@
 TAG_BITS = 8
 CHUNK = 4 * LANES
 PAIRED_MAX = 16
-CALLS = (0, 2, 4, 7, 8)
+CALLS = (0, 2, 5, 7, 8)
 VMEM_LIMIT = 48 * 1024 * 1024
 
 

time: 43.8 us -> 41.7 us (0.952)
  waiting for transfers between devices: 5.84 us -> 4.63 us
  starting transfers between devices: 17.5 us -> 16.7 us
    ppermute x7, waiting for transfers between devices: 4.99 us -> 3.78 us  [local(): piece = lax.ppermute(piece, ('blk', 'tile'), pairs)]
    ppermute x7, starting transfers between devices: 16.4 us -> 15.6 us  [local(): piece = lax.ppermute(piece, ('blk', 'tile'), pairs)]
  transfers between devices with their start and end apart: 10 -> 10, of which waited for: 4 -> 4; matrix products, arithmetic and copies ran while one was open for 2% -> 2% of each run, Pallas kernels for 29% -> 28%
where the time goes in v2:
time: 41.7 us; the launch traced here: 41.3 us
  Pallas kernels  17.1 us (41%)
  starting transfers between devices  16.7 us (40%)
  waiting for transfers between devices  4.63 us (11%)
  other arithmetic  2.06 us (5%)
  local copies, waits for them, and re-layouts  0.73 us (2%)
    ppermute x7, starting transfers between devices, local(): piece = lax.ppermute(piece, ('blk', 'tile'), pairs)  15.6 us
    pallas_call x4, Pallas kernels, make_subgrids(): pl.pallas_call(functools.partial(subgrid_kernel, first, destinations, cap...  13.9 us
    ppermute x7, waiting for transfers between devices, local(): piece = lax.ppermute(piece, ('blk', 'tile'), pairs)  3.78 us
    pallas_call x2, Pallas kernels, add_half(): pl.pallas_call(functools.partial(add_kernel, at), out_shape=jax.ShapeDtyp...  1.67 us
    add x1, other arithmetic, local(): own.astype(jnp.float32) + other.astype(jnp.float32)  1.22 us
  transfers between devices with their start and end apart: 10, of which 4 were waited for; matrix products, arithmetic and copies ran while one was open for 2% of the time, Pallas kernels for 28%

profile of v2, /device:TPU:0, one launch (start us, length us, event | category | flops | bytes accessed | tf_op | source)
XLA Modules:
  0.0 41.3 jit_solution(2633499970871623953)
XLA Ops:
  0.0 0.5 %collective-permute-start = (bf16[2048,128]{1,0:T(8,128)(2,1)}, bf16[2048,128]{1,0:T(8,128)(2,1)S(1)}, u32[]{:S(2)}, u32[]{:S(2)}) collective-permute-start(bf16[2048,128]{1,0:T(8,128)(2,1)} %bitcast.20), channel_id=1, source_target_pairs={{0,8},{8,0},{1,9},{9,1},{2,10},{10,2},{3,11},{11,3},{4,12},{12,4},... | collective-permute-start | bytes 1572872 | tf_op jit(solution)/shard_map/ppermute | solution.py:408
  0.5 0.0 copy-start.2
  0.5 0.0 copy-start.3
  0.5 0.0 copy-start.1
  0.5 0.0 copy-start.4
  0.5 0.7 %copy-done.2 = s32[256]{0:T(256)S(1)} copy-done((s32[256]{0:T(256)S(1)}, s32[256]{0:T(256)}, u32[]{:S(2)}) %copy-start.2) | copy-done | bytes 1048
  1.1 0.0 copy-done.3
  1.1 0.0 copy-done.1
  1.2 0.0 copy-done.4
  1.2 0.1 select_reduce_fusion.3
  1.3 0.2 convert_reduce_fusion
  1.5 0.1 convert_reduce_fusion.1
  1.6 0.1 select_reduce_fusion.2
  1.7 0.1 select_reduce_fusion.4
  1.8 0.2 select_reduce_fusion.1
  2.0 0.1 pad_add_fusion.1.plan_ref
  2.1 0.0 copy-start
  2.1 0.1 collective-permute-done
  2.2 1.2 %convert_add_fusion.res_ref = f32[2048,128]{1,0:T(8,128)S(1)} fusion(bf16[2048,128]{1,0:T(8,128)(2,1)S(1)} %collective-permute-done, bf16[2048,128]{1,0:T(8,128)(2,1)} %bitcast.21), kind=kLoop, calls=%fused_computation | loop fusion | flops 786432 | bytes 2097152 | tf_op jit(solution)/shard_map/add | solution.py:445
  3.4 0.0 copy-done
  3.4 4.0 %subgrids.4 = (bf16[528,128]{1,0:T(8,128)(2,1)S(1)}, bf16[528,128]{1,0:T(8,128)(2,1)S(1)}, s32[8,128]{1,0:T(8,128)S(1)}) custom-call(s32[329]{0:T(512)S(1)} %pad_add_fusion.1.plan_ref, s32[8,128]{1,0:T(8,128)S(1)} %broadcast_in_dim.115.token_ref, f32[2048,128]{1,0:T(8,128)S(1)} %bitcast.16, f32[2048,128]{1,0:T(8,128)S(1)} %convert_add_fusion.res_ref), custom_call_target="tpu_custom_call" | custom-call | flops 268435456 | bytes 524288 | tf_op jit(solution)/shard_map/subgrids/pallas_call | solution.py:256
  7.5 4.9 %collective-permute-start.1 = (bf16[528,128]{1,0:T(8,128)(2,1)S(1)}, bf16[528,128]{1,0:T(8,128)(2,1)S(1)}, u32[]{:S(2)}, u32[]{:S(2)}) collective-permute-start(bf16[528,128]{1,0:T(8,128)(2,1)S(1)} %get-tuple-element.19), channel_id=1, source_target_pairs={{0,7},{1,6},{2,5},{3,4},{4,3},{5,2},{6,1},{7,0},{8,15},{9,14},{10,... | collective-permute-start | bytes 405512 | tf_op jit(solution)/shard_map/ppermute | solution.py:459
  12.3 1.2 %collective-permute-start.2 = (bf16[528,128]{1,0:T(8,128)(2,1)S(1)}, bf16[528,128]{1,0:T(8,128)(2,1)S(1)}, u32[]{:S(2)}, u32[]{:S(2)}) collective-permute-start(bf16[528,128]{1,0:T(8,128)(2,1)S(1)} %get-tuple-element.20), channel_id=1, source_target_pairs={{0,6},{1,7},{2,4},{3,5},{4,2},{5,3},{6,0},{7,1},{8,14},{9,15},{10,... | collective-permute-start | bytes 405512 | tf_op jit(solution)/shard_map/ppermute | solution.py:459
  13.6 5.0 %subgrids.5 = (bf16[528,128]{1,0:T(8,128)(2,1)S(1)}, bf16[528,128]{1,0:T(8,128)(2,1)S(1)}, bf16[528,128]{1,0:T(8,128)(2,1)S(1)}, s32[8,128]{1,0:T(8,128)S(1)}) custom-call(s32[329]{0:T(512)S(1)} %pad_add_fusion.1.plan_ref, s32[8,128]{1,0:T(8,128)S(1)} %get-tuple-element.21.token_ref, f32[2048,128]{1,0:T(8,128)S(1)} %bitcast.17, ...), custom_call_target="tpu_custom_call" | custom-call | flops 402653184 | bytes 786432 | tf_op jit(solution)/shard_map/subgrids/pallas_call | solution.py:256
  18.6 0.1 collective-permute-start.3
  18.7 1.3 %collective-permute-start.4 = (bf16[528,128]{1,0:T(8,128)(2,1)S(1)}, bf16[528,128]{1,0:T(8,128)(2,1)S(1)}, u32[]{:S(2)}, u32[]{:S(2)}) collective-permute-start(bf16[528,128]{1,0:T(8,128)(2,1)S(1)} %get-tuple-element.23), channel_id=1, source_target_pairs={{0,4},{1,5},{2,6},{3,7},{4,0},{5,1},{6,2},{7,3},{8,12},{9,13},{10,... | collective-permute-start | bytes 405512 | tf_op jit(solution)/shard_map/ppermute | solution.py:459
  20.0 2.8 %collective-permute-start.5 = (bf16[528,128]{1,0:T(8,128)(2,1)S(1)}, bf16[528,128]{1,0:T(8,128)(2,1)S(1)}, u32[]{:S(2)}, u32[]{:S(2)}) collective-permute-start(bf16[528,128]{1,0:T(8,128)(2,1)S(1)} %get-tuple-element.24), channel_id=1, source_target_pairs={{0,3},{1,2},{2,1},{3,0},{4,7},{5,6},{6,5},{7,4},{8,11},{9,10},{10,... | collective-permute-start | bytes 405512 | tf_op jit(solution)/shard_map/ppermute | solution.py:459
  22.8 2.5 %subgrids.6 = (bf16[528,128]{1,0:T(8,128)(2,1)S(1)}, bf16[528,128]{1,0:T(8,128)(2,1)S(1)}, s32[8,128]{1,0:T(8,128)S(1)}) custom-call(s32[329]{0:T(512)S(1)} %pad_add_fusion.1.plan_ref, s32[8,128]{1,0:T(8,128)S(1)} %get-tuple-element.25.token_ref, f32[2048,128]{1,0:T(8,128)S(1)} %bitcast.18, f32[2048,128]{1,0:T(8,128)S(1)} %convert_add_fusion.res_ref), custom_call_target="tpu_custom_call" | custom-call | flops 268435456 | bytes 524288 | tf_op jit(solution)/shard_map/subgrids/pallas_call | solution.py:256
  25.3 0.0 collective-permute-done.1.refs_0_
  25.3 2.3 %collective-permute-start.6 = (bf16[528,128]{1,0:T(8,128)(2,1)S(1)}, bf16[528,128]{1,0:T(8,128)(2,1)S(1)}, u32[]{:S(2)}, u32[]{:S(2)}) collective-permute-start(bf16[528,128]{1,0:T(8,128)(2,1)S(1)} %get-tuple-element.26), channel_id=1, source_target_pairs={{0,2},{1,3},{2,0},{3,1},{4,6},{5,7},{6,4},{7,5},{8,10},{9,11},{10,... | collective-permute-start | bytes 405512 | tf_op jit(solution)/shard_map/ppermute | solution.py:459
  27.6 0.0 collective-permute-done.2.refs_1_
  27.6 3.0 %collective-permute-start.7 = (bf16[528,128]{1,0:T(8,128)(2,1)S(1)}, bf16[528,128]{1,0:T(8,128)(2,1)S(1)}, u32[]{:S(2)}, u32[]{:S(2)}) collective-permute-start(bf16[528,128]{1,0:T(8,128)(2,1)S(1)} %get-tuple-element.27), channel_id=1, source_target_pairs={{0,1},{1,0},{2,3},{3,2},{4,5},{5,4},{6,7},{7,6},{8,9},{9,8},{10,11... | collective-permute-start | bytes 405512 | tf_op jit(solution)/shard_map/ppermute | solution.py:459
  30.6 2.4 %subgrids.7 = (bf16[528,128]{1,0:T(8,128)(2,1)S(1)}, s32[8,128]{1,0:T(8,128)}) custom-call(s32[329]{0:T(512)S(1)} %pad_add_fusion.1.plan_ref, s32[8,128]{1,0:T(8,128)S(1)} %get-tuple-element.28.token_ref, f32[2048,128]{1,0:T(8,128)S(1)} %bitcast.19, f32[2048,128]{1,0:T(8,128)S(1)} %convert_add_fusion.res_ref), custom_call_target="tpu_custom_call" | custom-call | flops 134217728 | bytes 262144 | tf_op jit(solution)/shard_map/subgrids/pallas_call | solution.py:256
  33.0 0.8 %collective-permute-done.3.refs_2_ = bf16[528,128]{1,0:T(8,128)(2,1)S(1)} collective-permute-done((bf16[528,128]{1,0:T(8,128)(2,1)S(1)}, bf16[528,128]{1,0:T(8,128)(2,1)S(1)}, u32[]{:S(2)}, u32[]{:S(2)}) %collective-permute-start.3) | collective-permute-done | bytes 135200 | tf_op jit(solution)/shard_map/ppermute | solution.py:459
  33.8 3.0 %collective-permute-done.4.refs_3_ = bf16[528,128]{1,0:T(8,128)(2,1)S(1)} collective-permute-done((bf16[528,128]{1,0:T(8,128)(2,1)S(1)}, bf16[528,128]{1,0:T(8,128)(2,1)S(1)}, u32[]{:S(2)}, u32[]{:S(2)}) %collective-permute-start.4) | collective-permute-done | bytes 135200 | tf_op jit(solution)/shard_map/ppermute | solution.py:459
  36.8 0.0 collective-permute-done.5.refs_4_
  36.8 0.0 collective-permute-done.6.refs_5_
  36.8 0.0 collective-permute-done.7.refs_6_
  36.8 0.8 %sum_first.1 = (f32[1024,128]{1,0:T(8,128)S(1)}, bf16[16,256,128]{2,1,0:T(8,128)(2,1)S(1)}, bf16[128,256]{1,0:T(8,128)(2,1)S(1)}) custom-call(bf16[528,128]{1,0:T(8,128)(2,1)S(1)} %collective-permute-done.1.refs_0_, bf16[528,128]{1,0:T(8,128)(2,1)S(1)} %collective-permute-done.2.refs_1_, bf16[528,128]{1,0:T(8,128)(2,1)S(1)} %collective-permute-done.3.refs_2_, ...), custom_call_target="tpu_custom_call" | custom-call | tf_op jit(solution)/shard_map/sum_first/pallas_call | solution.py:330
  37.6 0.1 collective-permute-start.9
  37.7 0.6 %sum_second.1.mine_ref = f32[1024,128]{1,0:T(8,128)S(1)} custom-call(bf16[16,256,128]{2,1,0:T(8,128)(2,1)S(1)} %get-tuple-element.30.xs, bf16[128,256]{1,0:T(8,128)(2,1)S(1)} %get-tuple-element.31.hot), custom_call_target="tpu_custom_call" | custom-call | tf_op jit(solution)/shard_map/sum_second/pallas_call | solution.py:343
  38.3 0.6 %collective-permute-start.8 = (f32[1024,128]{1,0:T(8,128)S(1)}, f32[1024,128]{1,0:T(8,128)S(1)}, u32[]{:S(2)}, u32[]{:S(2)}) collective-permute-start(f32[1024,128]{1,0:T(8,128)S(1)} %sum_second.1.mine_ref), channel_id=1, source_target_pairs={{0,8},{8,0},{1,9},{9,1},{2,10},{10,2},{3,11},{11,3},{4,12},{12,4},... | collective-permute-start | bytes 1572872 | tf_op jit(solution)/shard_map/ppermute | solution.py:469
  38.9 0.7 %collective-permute-done.9.theirs_ref = f32[1024,128]{1,0:T(8,128)S(1)} collective-permute-done((f32[1024,128]{1,0:T(8,128)S(1)}, f32[1024,128]{1,0:T(8,128)S(1)}, u32[]{:S(2)}, u32[]{:S(2)}) %collective-permute-start.9) | collective-permute-done | bytes 524320 | tf_op jit(solution)/shard_map/ppermute | solution.py:468
  39.6 0.8 %add_half.2.refs_0_ = f32[2048,128]{1,0:T(8,128)} custom-call(f32[1024,128]{1,0:T(8,128)S(1)} %get-tuple-element.32.mine_ref, f32[1024,128]{1,0:T(8,128)S(1)} %collective-permute-done.9.theirs_ref), custom_call_target="tpu_custom_call" | custom-call | tf_op jit(solution)/shard_map/add_half/pallas_call | solution.py:373
  40.4 0.0 collective-permute-done.8.theirs_ref
  40.5 0.8 %add_half.3 = f32[2048,128]{1,0:T(8,128)} custom-call(f32[1024,128]{1,0:T(8,128)S(1)} %sum_second.1.mine_ref, f32[1024,128]{1,0:T(8,128)S(1)} %collective-permute-done.8.theirs_ref, f32[2048,128]{1,0:T(8,128)} %add_half.2.refs_0_), custom_call_target="tpu_custom_call", output_to_operand_aliasing={{}: (2, {})} | custom-call | tf_op jit(solution)/shard_map/add_half/pallas_call | solution.py:373
  (8 shorter events, 0.1 us)
Async XLA Ops:
  0.0 2.2 %collective-permute-start = (bf16[2048,128]{1,0:T(8,128)(2,1)}, bf16[2048,128]{1,0:T(8,128)(2,1)S(1)}, u32[]{:S(2)}, u32[]{:S(2)}) collective-permute-start(bf16[2048,128]{1,0:T(8,128)(2,1)} %bitcast.20), channel_id=1, source_target_pairs={{0,8},{8,0},{1,9},{9,1},{2,10},{10,2},{3,11},{11,3},{4,12},{12,4},... | collective-permute-start | bytes 1572872 | tf_op jit(solution)/shard_map/ppermute | solution.py:408
  0.5 0.7 %copy-start.2 = (s32[256]{0:T(256)S(1)}, s32[256]{0:T(256)}, u32[]{:S(2)}) copy-start(s32[256]{0:T(256)} %param.10) | copy-start | bytes 3076
  0.5 0.7 %copy-start.3 = (s32[256,1]{0,1:T(1,128)S(1)}, s32[256,1]{0,1:T(1,128)}, u32[]{:S(2)}) copy-start(s32[256,1]{0,1:T(1,128)} %param.9) | copy-start | bytes 3076
  0.5 0.7 %copy-start.1 = (s32[256]{0:T(256)S(1)}, s32[256]{0:T(256)}, u32[]{:S(2)}) copy-start(s32[256]{0:T(256)} %param.8) | copy-start | bytes 3076
  0.5 0.7 %copy-start.4 = (s32[8]{0:T(128)S(1)}, s32[8]{0:T(128)}, u32[]{:S(2)}) copy-start(s32[8]{0:T(128)} %param.11) | copy-start | bytes 100
  2.1 1.4 %copy-start = (f32[256,2,512]{2,1,0:T(2,128)S(1)}, f32[256,2,512]{2,1,0:T(2,128)}, u32[]{:S(2)}) copy-start(f32[256,2,512]{2,1,0:T(2,128)} %param.7) | copy-start | bytes 3145732
  7.5 17.9 %collective-permute-start.1 = (bf16[528,128]{1,0:T(8,128)(2,1)S(1)}, bf16[528,128]{1,0:T(8,128)(2,1)S(1)}, u32[]{:S(2)}, u32[]{:S(2)}) collective-permute-start(bf16[528,128]{1,0:T(8,128)(2,1)S(1)} %get-tuple-element.19), channel_id=1, source_target_pairs={{0,7},{1,6},{2,5},{3,4},{4,3},{5,2},{6,1},{7,0},{8,15},{9,14},{10,... | collective-permute-start | bytes 405512 | tf_op jit(solution)/shard_map/ppermute | solution.py:459
  12.3 15.3 %collective-permute-start.2 = (bf16[528,128]{1,0:T(8,128)(2,1)S(1)}, bf16[528,128]{1,0:T(8,128)(2,1)S(1)}, u32[]{:S(2)}, u32[]{:S(2)}) collective-permute-start(bf16[528,128]{1,0:T(8,128)(2,1)S(1)} %get-tuple-element.20), channel_id=1, source_target_pairs={{0,6},{1,7},{2,4},{3,5},{4,2},{5,3},{6,0},{7,1},{8,14},{9,15},{10,... | collective-permute-start | bytes 405512 | tf_op jit(solution)/shard_map/ppermute | solution.py:459
  18.6 15.2 %collective-permute-start.3 = (bf16[528,128]{1,0:T(8,128)(2,1)S(1)}, bf16[528,128]{1,0:T(8,128)(2,1)S(1)}, u32[]{:S(2)}, u32[]{:S(2)}) collective-permute-start(bf16[528,128]{1,0:T(8,128)(2,1)S(1)} %get-tuple-element.22), channel_id=1, source_target_pairs={{0,5},{1,4},{2,7},{3,6},{4,1},{5,0},{6,3},{7,2},{8,13},{9,12},{10,... | collective-permute-start | bytes 405512 | tf_op jit(solution)/shard_map/ppermute | solution.py:459
  18.7 18.1 %collective-permute-start.4 = (bf16[528,128]{1,0:T(8,128)(2,1)S(1)}, bf16[528,128]{1,0:T(8,128)(2,1)S(1)}, u32[]{:S(2)}, u32[]{:S(2)}) collective-permute-start(bf16[528,128]{1,0:T(8,128)(2,1)S(1)} %get-tuple-element.23), channel_id=1, source_target_pairs={{0,4},{1,5},{2,6},{3,7},{4,0},{5,1},{6,2},{7,3},{8,12},{9,13},{10,... | collective-permute-start | bytes 405512 | tf_op jit(solution)/shard_map/ppermute | solution.py:459
  20.0 16.8 %collective-permute-start.5 = (bf16[528,128]{1,0:T(8,128)(2,1)S(1)}, bf16[528,128]{1,0:T(8,128)(2,1)S(1)}, u32[]{:S(2)}, u32[]{:S(2)}) collective-permute-start(bf16[528,128]{1,0:T(8,128)(2,1)S(1)} %get-tuple-element.24), channel_id=1, source_target_pairs={{0,3},{1,2},{2,1},{3,0},{4,7},{5,6},{6,5},{7,4},{8,11},{9,10},{10,... | collective-permute-start | bytes 405512 | tf_op jit(solution)/shard_map/ppermute | solution.py:459
  25.3 11.5 %collective-permute-start.6 = (bf16[528,128]{1,0:T(8,128)(2,1)S(1)}, bf16[528,128]{1,0:T(8,128)(2,1)S(1)}, u32[]{:S(2)}, u32[]{:S(2)}) collective-permute-start(bf16[528,128]{1,0:T(8,128)(2,1)S(1)} %get-tuple-element.26), channel_id=1, source_target_pairs={{0,2},{1,3},{2,0},{3,1},{4,6},{5,7},{6,4},{7,5},{8,10},{9,11},{10,... | collective-permute-start | bytes 405512 | tf_op jit(solution)/shard_map/ppermute | solution.py:459
  27.6 9.2 %collective-permute-start.7 = (bf16[528,128]{1,0:T(8,128)(2,1)S(1)}, bf16[528,128]{1,0:T(8,128)(2,1)S(1)}, u32[]{:S(2)}, u32[]{:S(2)}) collective-permute-start(bf16[528,128]{1,0:T(8,128)(2,1)S(1)} %get-tuple-element.27), channel_id=1, source_target_pairs={{0,1},{1,0},{2,3},{3,2},{4,5},{5,4},{6,7},{7,6},{8,9},{9,8},{10,11... | collective-permute-start | bytes 405512 | tf_op jit(solution)/shard_map/ppermute | solution.py:459
  37.6 2.0 %collective-permute-start.9 = (f32[1024,128]{1,0:T(8,128)S(1)}, f32[1024,128]{1,0:T(8,128)S(1)}, u32[]{:S(2)}, u32[]{:S(2)}) collective-permute-start(f32[1024,128]{1,0:T(8,128)S(1)} %get-tuple-element.32.mine_ref), channel_id=1, source_target_pairs={{0,8},{8,0},{1,9},{9,1},{2,10},{10,2},{3,11},{11,3},{4,12},{12,4},... | collective-permute-start | bytes 1572872 | tf_op jit(solution)/shard_map/ppermute | solution.py:468
  38.3 2.1 %collective-permute-start.8 = (f32[1024,128]{1,0:T(8,128)S(1)}, f32[1024,128]{1,0:T(8,128)S(1)}, u32[]{:S(2)}, u32[]{:S(2)}) collective-permute-start(f32[1024,128]{1,0:T(8,128)S(1)} %sum_second.1.mine_ref), channel_id=1, source_target_pairs={{0,8},{8,0},{1,9},{9,1},{2,10},{10,2},{3,11},{11,3},{4,12},{12,4},... | collective-permute-start | bytes 1572872 | tf_op jit(solution)/shard_map/ppermute | solution.py:469
